TPU v7x, 256 devices: a whole 4x4x8 slice. The times are simulated.
256 devices in a mesh: dp: 16 (over y_lo, x, core), shard: 16 (over z, y_hi).
Axes of the slice: x: 4, y: 4 (y_hi: 2, y_lo: 2; y = y_hi * 2 + y_lo), z: 8, core: 2. Of those that a mesh axis runs over, the one named last changes fastest.
Arguments:
- points: bfloat16 [32768, 256], P(('dp', 'shard')), may hold values from -48 to 48
- codebook: float32 [65536, 256], P('shard'), may hold values from -5 to 5
Outputs:
- updated: float32 [65536, 256], P('shard')
- log_partition: float32 [32768], P(('dp', 'shard'))
All inputs are finite; a program needn't handle non-finite values.
Results may differ from a plain program's by a relative error of at most 0.0063.
Values may be sent and summed in bfloat16 or wider, within the bound.
A program may use at most 128 MiB of HBM per device.

v0:
```python
import math

import jax
import jax.numpy as jnp
from jax import lax
from jax.sharding import PartitionSpec as P


def shards(points, codebook):
    gathered = lax.all_gather(points, "shard", axis=0, tiled=True)
    feature_count = codebook.shape[1]
    sharpness = 4.0 / math.sqrt(feature_count)
    narrow = codebook.astype(jnp.bfloat16)
    half_norm = 0.5 * jnp.sum(codebook * codebook, axis=1)
    row_count = gathered.shape[0]
    row_span = min(512, row_count)
    blocked = gathered.reshape(row_count // row_span, row_span, feature_count)

    def local_stats(block_rows):
        inner = lax.dot_general(
            block_rows, narrow, (((1,), (1,)), ((), ())), preferred_element_type=jnp.float32
        )
        scores = sharpness * (inner - half_norm[None, :])
        row_peak = jnp.max(scores, axis=1)
        return (scores, row_peak, jnp.sum(jnp.exp(scores - row_peak[:, None]), axis=1))

    kept_scores, row_peaks, totals = lax.map(local_stats, blocked)
    global_peak = lax.pmax(row_peaks, "shard")
    global_total = lax.psum(totals * jnp.exp(row_peaks - global_peak), "shard")
    logsums = global_peak + jnp.log(global_total)

    def advance(running, operands):
        centroid_sums, masses = running
        block_rows, block_scores, block_logsum = operands
        assigned = jnp.exp(block_scores - block_logsum[:, None]).astype(jnp.bfloat16)
        centroid_sums = centroid_sums + lax.dot_general(
            assigned, block_rows, (((0,), (0,)), ((), ())), preferred_element_type=jnp.float32
        )
        masses = masses + jnp.sum(assigned.astype(jnp.float32), axis=0)
        return ((centroid_sums, masses), None)

    start = (jnp.zeros(codebook.shape, jnp.float32), jnp.zeros((codebook.shape[0],), jnp.float32))
    (centroid_sums, masses), unused = lax.scan(advance, start, (blocked, kept_scores, logsums))
    total_sums, total_masses = lax.psum((centroid_sums, masses), "dp")
    updated = (total_sums + codebook) / (total_masses[:, None] + 1.0)
    own_rows = points.shape[0]
    flattened = logsums.reshape(row_count)
    own_logsum = lax.dynamic_slice_in_dim(
        flattened, lax.axis_index("shard") * own_rows, own_rows, 0
    )
    return (updated, own_logsum)


def solution(mesh):
    in_specs = (P(("dp", "shard"), None), P("shard", None))
    out_specs = (P("shard", None), P(("dp", "shard")))
    return jax.shard_map(shards, mesh=mesh, in_specs=in_specs, out_specs=out_specs, check_vma=False)
```

profile of v0, /device:TPU:1, one launch (start us, length us, event | category | flops | bytes accessed | tf_op | source)
XLA Modules:
  0.0 434.2 jit_solution(9917395567991500416)
XLA Ops:
  7.2 0.0 all-gather.2.cloned.1.call-start
  7.2 0.7 all-gather.2.cloned.1.call-update
  7.9 0.0 all-reduce.2.cloned.1.call-start
  8.0 4.3 multiply_reduce_fusion
  12.3 77.2 %all-gather.2.cloned.1.call-done = bf16[2048,256]{1,0:T(8,128)(2,1)} async-done(((bf16[128,256]{1,0:T(8,128)(2,1)}), bf16[2048,256]{1,0:T(8,128)(2,1)}) %all-gather.2.cloned.1.call-update) | async-done | bytes 1048592 | tf_op jit(solution)/shard_map/all_gather | solution.py:10
  89.5 66.2 %while.27 = (s32[]{:T(128)}, f32[4,512,4096]{2,1,0:T(8,128)}, f32[4,512]{1,0:T(4,128)S(1)}, f32[4,512]{1,0:T(4,128)S(1)}, bf16[4,512,256]{2,1,0:T(8,128)(2,1)}, ...) while((s32[]{:T(128)}, f32[4,512,4096]{2,1,0:T(8,128)}, ...), condition=%wide.region_4.5_spmd, body=%wide.region_1.4_spmd.sunk | while | flops 1084226560 | bytes 35945584 | solution.py:27
  89.5 8.0 %bitcast_dynamic-update-slice_fusion.2 = (f32[4,512,4096]{2,1,0:T(8,128)}, f32[512,4096]{1,0:T(8,128)}) fusion(f32[4,512,4096]{2,1,0:T(8,128)} %get-tuple-element.225, s32[]{:T(128)} %get-tuple-element.224, f32[4096]{0:T(1024)S(1)} %get-tuple-element.240, bf16[4096,256]{1,0:T(8,128)(2,1)S(1)} %get-tuple-element.239, ...), kind=kOutput, calls=%fused_computation.clone.1 | convolution fusion | flops 1077936128 | bytes 19153920 | tf_op jit(solution)/shard_map/while/body/eval_jaxpr/dot_general | solution.py:20
  97.5 3.8 reduce_max.10
  101.3 4.6 %exponential_reduce_fusion.2 = f32[512]{0:T(512)S(1)} fusion(f32[512,4096]{1,0:T(8,128)} %get-tuple-element.207, f32[512]{0:T(512)S(1)} %reduce_max.10), kind=kLoop, calls=%fused_computation.1.clone.1 | loop fusion | flops 4193792 | bytes 8392704 | tf_op jit(solution)/shard_map/while/body/eval_jaxpr/reduce_sum | solution.py:25
  106.0 0.1 dynamic_update_slice.16
  106.1 8.0 %bitcast_dynamic-update-slice_fusion.2 = (f32[4,512,4096]{2,1,0:T(8,128)}, f32[512,4096]{1,0:T(8,128)}) fusion(f32[4,512,4096]{2,1,0:T(8,128)} %get-tuple-element.225, s32[]{:T(128)} %get-tuple-element.224, f32[4096]{0:T(1024)S(1)} %get-tuple-element.240, bf16[4096,256]{1,0:T(8,128)(2,1)S(1)} %get-tuple-element.239, ...), kind=kOutput, calls=%fused_computation.clone.1 | convolution fusion | flops 1077936128 | bytes 19153920 | tf_op jit(solution)/shard_map/while/body/eval_jaxpr/dot_general | solution.py:20
  114.0 3.8 reduce_max.10
  117.9 4.6 %exponential_reduce_fusion.2 = f32[512]{0:T(512)S(1)} fusion(f32[512,4096]{1,0:T(8,128)} %get-tuple-element.207, f32[512]{0:T(512)S(1)} %reduce_max.10), kind=kLoop, calls=%fused_computation.1.clone.1 | loop fusion | flops 4193792 | bytes 8392704 | tf_op jit(solution)/shard_map/while/body/eval_jaxpr/reduce_sum | solution.py:25
  122.5 0.1 dynamic_update_slice.16
  122.6 8.0 %bitcast_dynamic-update-slice_fusion.2 = (f32[4,512,4096]{2,1,0:T(8,128)}, f32[512,4096]{1,0:T(8,128)}) fusion(f32[4,512,4096]{2,1,0:T(8,128)} %get-tuple-element.225, s32[]{:T(128)} %get-tuple-element.224, f32[4096]{0:T(1024)S(1)} %get-tuple-element.240, bf16[4096,256]{1,0:T(8,128)(2,1)S(1)} %get-tuple-element.239, ...), kind=kOutput, calls=%fused_computation.clone.1 | convolution fusion | flops 1077936128 | bytes 19153920 | tf_op jit(solution)/shard_map/while/body/eval_jaxpr/dot_general | solution.py:20
  130.6 3.8 reduce_max.10
  134.4 4.6 %exponential_reduce_fusion.2 = f32[512]{0:T(512)S(1)} fusion(f32[512,4096]{1,0:T(8,128)} %get-tuple-element.207, f32[512]{0:T(512)S(1)} %reduce_max.10), kind=kLoop, calls=%fused_computation.1.clone.1 | loop fusion | flops 4193792 | bytes 8392704 | tf_op jit(solution)/shard_map/while/body/eval_jaxpr/reduce_sum | solution.py:25
  139.1 0.1 dynamic_update_slice.16
  139.2 8.0 %bitcast_dynamic-update-slice_fusion.2 = (f32[4,512,4096]{2,1,0:T(8,128)}, f32[512,4096]{1,0:T(8,128)}) fusion(f32[4,512,4096]{2,1,0:T(8,128)} %get-tuple-element.225, s32[]{:T(128)} %get-tuple-element.224, f32[4096]{0:T(1024)S(1)} %get-tuple-element.240, bf16[4096,256]{1,0:T(8,128)(2,1)S(1)} %get-tuple-element.239, ...), kind=kOutput, calls=%fused_computation.clone.1 | convolution fusion | flops 1077936128 | bytes 19153920 | tf_op jit(solution)/shard_map/while/body/eval_jaxpr/dot_general | solution.py:20
  147.1 3.8 reduce_max.10
  151.0 4.6 %exponential_reduce_fusion.2 = f32[512]{0:T(512)S(1)} fusion(f32[512,4096]{1,0:T(8,128)} %get-tuple-element.207, f32[512]{0:T(512)S(1)} %reduce_max.10), kind=kLoop, calls=%fused_computation.1.clone.1 | loop fusion | flops 4193792 | bytes 8392704 | tf_op jit(solution)/shard_map/while/body/eval_jaxpr/reduce_sum | solution.py:25
  155.7 0.1 dynamic_update_slice.16
  155.7 31.6 %pmax.7 = f32[4,512]{1,0:T(4,128)S(1)} all-reduce(f32[4,512]{1,0:T(4,128)S(1)} %get-tuple-element.75), channel_id=1, replica_groups=mesh['dp'=16,'shard'=16] {'shard'}, use_global_device_ids=true, to_apply=%region_5.6 | all-reduce | flops 2048 | bytes 16384 | tf_op jit(solution)/shard_map/pmax | solution.py:28
  187.4 32.0 %psum.21 = f32[4,512]{1,0:T(4,128)S(1)} all-reduce(f32[4,512]{1,0:T(4,128)S(1)} %exponential_multiply_fusion), channel_id=1, replica_groups=mesh['dp'=16,'shard'=16] {'shard'}, use_global_device_ids=true, to_apply=%region_6.7 | all-reduce | flops 2048 | bytes 16384 | tf_op jit(solution)/shard_map/psum | solution.py:29
  219.4 52.2 %while.28 = (s32[]{:T(128)}, f32[4096,256]{1,0:T(8,128)}, f32[4096]{0:T(1024)S(1)}, f32[4,512,4096]{2,1,0:T(8,128)}, f32[4,512]{1,0:T(4,128)S(1)}, /*index=5*/bf16[4,512,256]{2,1,0:T(8,128)(2,1)}, s32[]{:T(128)}, s32[]{:T(128)}) while((s32[]{:T(128)}, f32[4096,256]{1,0:T(8,128)}, f32[4096]{0:T(1024)S(1)}, ...), condition=%wide.region_9.10_spmd.clone, body=%wide.region_7.9_spmd.clone.sunk | while | flops 1088425984 | bytes 25502820 | solution.py:43
  219.4 7.3 %convolution_add_fusion.2 = f32[4096,256]{1,0:T(8,128)} fusion(f32[4,512,4096]{2,1,0:T(8,128)} %get-tuple-element.263, s32[]{:T(128)} %get-tuple-element.252, f32[4096,256]{1,0:T(8,128)} %get-tuple-element.253, f32[512]{0:T(512)S(1)} %bitcast.48, pred[]{:T(512)S(6)} %compare.3, bf16[4,512,256]{2,1,0:T(8,128)(2,1)} %get-tuple-element.265), kind=kOutput, calls=%fused_computation.11.clone.1 | convolution fusion | flops 1080033280 | bytes 17042432 | tf_op jit(solution)/shard_map/while/body/eval_jaxpr/dot_general | solution.py:36
  226.7 4.7 %convert_reduce_fusion.2 = f32[4096]{0:T(1024)S(1)} fusion(f32[4,512,4096]{2,1,0:T(8,128)} %get-tuple-element.263, s32[]{:T(128)} %get-tuple-element.252, f32[512]{0:T(512)S(1)} %bitcast.49), kind=kLoop, calls=%fused_computation.9.clone.1 | loop fusion | flops 8384512 | bytes 8407044 | tf_op jit(solution)/shard_map/while/body/eval_jaxpr/reduce_sum | solution.py:39
  231.5 8.6 %convolution_add_fusion.2 = f32[4096,256]{1,0:T(8,128)} fusion(f32[4,512,4096]{2,1,0:T(8,128)} %get-tuple-element.263, s32[]{:T(128)} %get-tuple-element.252, f32[4096,256]{1,0:T(8,128)} %get-tuple-element.253, f32[512]{0:T(512)S(1)} %bitcast.48, pred[]{:T(512)S(6)} %compare.3, bf16[4,512,256]{2,1,0:T(8,128)(2,1)} %get-tuple-element.265), kind=kOutput, calls=%fused_computation.11.clone.1 | convolution fusion | flops 1080033280 | bytes 17042432 | tf_op jit(solution)/shard_map/while/body/eval_jaxpr/dot_general | solution.py:36
  240.1 4.7 %convert_reduce_fusion.2 = f32[4096]{0:T(1024)S(1)} fusion(f32[4,512,4096]{2,1,0:T(8,128)} %get-tuple-element.263, s32[]{:T(128)} %get-tuple-element.252, f32[512]{0:T(512)S(1)} %bitcast.49), kind=kLoop, calls=%fused_computation.9.clone.1 | loop fusion | flops 8384512 | bytes 8407044 | tf_op jit(solution)/shard_map/while/body/eval_jaxpr/reduce_sum | solution.py:39
  244.9 8.6 %convolution_add_fusion.2 = f32[4096,256]{1,0:T(8,128)} fusion(f32[4,512,4096]{2,1,0:T(8,128)} %get-tuple-element.263, s32[]{:T(128)} %get-tuple-element.252, f32[4096,256]{1,0:T(8,128)} %get-tuple-element.253, f32[512]{0:T(512)S(1)} %bitcast.48, pred[]{:T(512)S(6)} %compare.3, bf16[4,512,256]{2,1,0:T(8,128)(2,1)} %get-tuple-element.265), kind=kOutput, calls=%fused_computation.11.clone.1 | convolution fusion | flops 1080033280 | bytes 17042432 | tf_op jit(solution)/shard_map/while/body/eval_jaxpr/dot_general | solution.py:36
  253.5 4.7 %convert_reduce_fusion.2 = f32[4096]{0:T(1024)S(1)} fusion(f32[4,512,4096]{2,1,0:T(8,128)} %get-tuple-element.263, s32[]{:T(128)} %get-tuple-element.252, f32[512]{0:T(512)S(1)} %bitcast.49), kind=kLoop, calls=%fused_computation.9.clone.1 | loop fusion | flops 8384512 | bytes 8407044 | tf_op jit(solution)/shard_map/while/body/eval_jaxpr/reduce_sum | solution.py:39
  258.3 8.6 %convolution_add_fusion.2 = f32[4096,256]{1,0:T(8,128)} fusion(f32[4,512,4096]{2,1,0:T(8,128)} %get-tuple-element.263, s32[]{:T(128)} %get-tuple-element.252, f32[4096,256]{1,0:T(8,128)} %get-tuple-element.253, f32[512]{0:T(512)S(1)} %bitcast.48, pred[]{:T(512)S(6)} %compare.3, bf16[4,512,256]{2,1,0:T(8,128)(2,1)} %get-tuple-element.265), kind=kOutput, calls=%fused_computation.11.clone.1 | convolution fusion | flops 1080033280 | bytes 17042432 | tf_op jit(solution)/shard_map/while/body/eval_jaxpr/dot_general | solution.py:36
  266.8 4.7 %convert_reduce_fusion.2 = f32[4096]{0:T(1024)S(1)} fusion(f32[4,512,4096]{2,1,0:T(8,128)} %get-tuple-element.263, s32[]{:T(128)} %get-tuple-element.252, f32[512]{0:T(512)S(1)} %bitcast.49), kind=kLoop, calls=%fused_computation.9.clone.1 | loop fusion | flops 8384512 | bytes 8407044 | tf_op jit(solution)/shard_map/while/body/eval_jaxpr/reduce_sum | solution.py:39
  271.6 0.0 all-reduce.2.cloned.1.call-update
  271.6 0.6 dynamic_slice.20
  272.2 67.1 %psum.23 = f32[4096]{0:T(1024)S(1)} all-reduce(f32[4096]{0:T(1024)S(1)} %get-tuple-element.78), channel_id=1, replica_groups=mesh['dp'=16,'shard'=16] {'dp'}, use_global_device_ids=true, to_apply=%region_11.12 | all-reduce | flops 4096 | bytes 32768 | tf_op jit(solution)/shard_map/psum | solution.py:44
  339.3 82.9 %all-reduce.2.cloned.1.call-done = f32[4096,256]{1,0:T(8,128)} async-done(((f32[4096,256]{1,0:T(8,128)}), f32[4096,256]{1,0:T(8,128)}) %all-reduce.2.cloned.1.call-update) | async-done | bytes 4194320 | tf_op jit(solution)/shard_map/psum | solution.py:44
  422.2 5.1 %add_divide_fusion = f32[4096,256]{1,0:T(8,128)} fusion(f32[4096,256]{1,0:T(8,128)} %all-reduce.2.cloned.1.call-done, f32[4096,256]{1,0:T(8,128)} %param.7, f32[4096]{0:T(1024)S(1)} %broadcast_add_fusion), kind=kLoop, calls=%fused_computation.19 | loop fusion | flops 2097152 | bytes 12599296 | tf_op jit(solution)/shard_map/div | solution.py:45
  (22 shorter events, 0.3 us)
Async XLA Ops:
  7.2 82.3 %all-gather.2.cloned.1.call-start = ((), (), s32[]{:S(2)}) async-start(), calls=%async_computation | async-start | bytes 1114112 | tf_op jit(solution)/shard_map/all_gather | solution.py:10
  7.9 414.3 %all-reduce.2.cloned.1.call-start = ((), (), s32[]{:S(2)}) async-start(), calls=%async_computation.1 | async-start | bytes 8388608 | tf_op jit(solution)/shard_map/psum | solution.py:44
Sparse Core Ops, SparseCore 0:
  10.6 78.8 all-gather.1
  271.7 150.4 all-reduce.1
where the time goes:
time: 435 us; the launch traced here: 434 us
  waiting for transfers between devices  161 us (37%)
  blocking collectives  131 us (30%)
  matrix products  64.9 us (15%)
  other arithmetic  62.3 us (14%)
  between operations  14.2 us (3%)
    psum x1, waiting for transfers between devices, shards(): total_sums, total_masses = lax.psum((centroid_sums, masses), 'dp')  82.9 us
    all_gather x1, waiting for transfers between devices, shards(): gathered = lax.all_gather(points, 'shard', axis=0, tiled=True)  77.2 us
    psum x1, blocking collectives, shards(): total_sums, total_masses = lax.psum((centroid_sums, masses), 'dp')  67.1 us
    dot_general x4, matrix products, advance(): lax.dot_general(assigned, block_rows, (((0,), (0,)), ((), ())), preferred...  33 us
    psum x1, blocking collectives, shards(): global_total = lax.psum(totals * jnp.exp(row_peaks - global_peak), 'shard')  32 us
    dot_general x4, matrix products, local_stats(): lax.dot_general(block_rows, narrow, (((1,), (1,)), ((), ())), preferred_e...  31.9 us
    pmax x1, blocking collectives, shards(): global_peak = lax.pmax(row_peaks, 'shard')  31.6 us
    reduce_sum x4, other arithmetic, advance(): masses = masses + jnp.sum(assigned.astype(jnp.float32), axis=0)  19 us
  transfers between devices with their start and end apart: 2, of which 2 were waited for; matrix products, arithmetic and copies ran while one was open for 1% of the time, Pallas kernels for 0%

commit v1 on v0

v1 whole, which is shorter than its diff:
```python
import functools
import math

import jax
import jax.numpy as jnp
from jax import lax
from jax.experimental import pallas as pl
from jax.experimental.pallas import tpu as pltpu
from jax.sharding import PartitionSpec as P

MESH = pl.DeviceIdType.MESH
BF = jnp.bfloat16
F32 = jnp.float32
W = 256
K = 4096
RB = 128
GR = 2 * RB
R = 16 * RB
KC = 512
CH = 256
SHARP = 4.0 / math.sqrt(W)
C2 = SHARP / math.log(2.0)

NAMES = (
    ["p_y0", "p_z1", "p_z7", "p_z2", "p_z6", "p_z3", "p_z5", "p_z4a", "p_z4b", "p_q1", "p_q7"]
    + ["p_y2", "p_y6", "p_y3", "p_y5", "p_y4a", "p_y4b"]
    + [f"s_{a}{b}" for a in range(8) for b in range(2) if a or b]
    + [f"h_{a}{b}" for a in range(2) for b in range(4)]
    + [f"n_{a}{b}" for a in range(2) for b in range(4)]
    + ["r_12", "r_11", "r_13", "r_a", "r_b", "r_y", "r_p", "r_m"]
    + ["g_p", "g_m", "g_y", "g_a", "g_b", "g_11", "g_13", "g_ya", "g_yb"]
    + [f"t_{a}" for a in ("00", "01", "03", "10", "2a", "2b", "11", "13", "12a", "12b")]
)
INDEX = {name: i for i, name in enumerate(NAMES)}
ORDER = (0, 1, 7, 2, 6, 3, 5, 4)


def encode(value):
    return (value * jnp.abs(value)) * (value * value)


def decode(power):
    size = jnp.abs(power)
    root = lax.rsqrt(lax.rsqrt(jnp.maximum(size, 1e-37)))
    root = jnp.where(size < 1e-37, 0.0, root)
    return jnp.where(power < 0.0, -root, root)


def kernel(
    points, codebook, out, lse_out,
    cb, narrow, norm, pbuf, pf, fl, scores, ebuf, peaks, mine, stats, lse_abs, fpad, part, hpart, mpart, hmass,
    nmass, message, inbox, cb_sem, send_sem, recv_sem,
):
    dp, shard = lax.axis_index("dp"), lax.axis_index("shard")
    ylo, x, core = dp // 8, (dp // 2) % 4, dp % 2
    z, yhi = shard // 2, shard % 2

    def peer(dyl=0, dx=0, dc=0, dz=0, dyh=0):
        return {
            "dp": ((ylo + dyl) % 2) * 8 + ((x + dx + 4) % 4) * 2 + (core + dc) % 2,
            "shard": ((z + dz + 8) % 8) * 2 + (yhi + dyh) % 2,
        }

    barrier = pltpu.get_barrier_semaphore()
    others = [peer(dz=a, dyh=b) for a in range(8) for b in range(2) if a or b]
    others += [peer(dx=1), peer(dx=-1), peer(dyl=1), peer(dc=1)]
    for other in others:
        pl.semaphore_signal(barrier, inc=1, device_id=other, device_id_type=MESH)

    loads = []
    for i in range(4):
        rows = pl.ds(i * (K // 4), K // 4)
        loads.append(pltpu.make_async_copy(codebook.at[rows], cb.at[rows], cb_sem.at[i]))
        loads[-1].start()
    pbuf[0, 0:RB, :] = points[...]
    for i in range(4):
        loads[i].wait()

        def prepare(j, unused, i=i):
            rows = pl.ds(pl.multiple_of(i * (K // 4) + j * 256, 256), 256)
            value = cb[rows, :]
            narrow[rows, :] = value.astype(BF)
            half = 0.5 * jnp.sum(value * value, axis=1, keepdims=True)
            norm[rows, :] = jnp.broadcast_to(half, (256, 128))
            return unused

        lax.fori_loop(0, K // 4 // 256, prepare, 0)

    pl.semaphore_wait(barrier, len(others))

    sent = {}

    def copy(name, src, dst, device):
        i = INDEX[name]
        return pltpu.make_async_remote_copy(
            src_ref=src, dst_ref=dst, send_sem=send_sem.at[i], recv_sem=recv_sem.at[i],
            device_id=device, device_id_type=MESH,
        )

    def send(name, src, dst, device):
        sent[name] = copy(name, src, dst, device)
        sent[name].start()

    def await_(name, dst):
        copy(name, dst, dst, peer(dc=1)).wait_recv()

    def block(dz, dy, half=None):
        if half is None:
            return pbuf.at[dz % 8, pl.ds(dy * RB, RB)]
        return pbuf.at[dz % 8, pl.ds(dy * RB + half * (RB // 2), RB // 2)]

    own = block(0, 0)
    send("p_y0", own, block(0, 1), peer(dyh=1))
    send("p_z1", own, block(1, 0), peer(dz=-1))
    send("p_z7", own, block(7, 0), peer(dz=1))
    send("p_z2", own, block(2, 0), peer(dz=-2))
    send("p_z6", own, block(6, 0), peer(dz=2))

    def arrive(g):
        if g == 0:
            await_("p_y0", block(0, 1))
            send("p_q1", block(0, 1), block(1, 1), peer(dz=-1))
            send("p_q7", block(0, 1), block(7, 1), peer(dz=1))
        elif g == 1:
            await_("p_z1", block(1, 0))
            await_("p_z7", block(7, 0))
            await_("p_z2", block(2, 0))
            send("p_z3", block(2, 0), block(3, 0), peer(dz=-1))
            send("p_y2", block(2, 0), block(2, 1), peer(dyh=1))
            await_("p_z6", block(6, 0))
            send("p_z5", block(6, 0), block(5, 0), peer(dz=1))
            send("p_y6", block(6, 0), block(6, 1), peer(dyh=1))
            await_("p_q1", block(1, 1))
        elif g == 7:
            await_("p_q7", block(7, 1))
        elif g == 2:
            await_("p_z3", block(3, 0))
            send("p_z4a", block(3, 0, 0), block(4, 0, 0), peer(dz=-1))
            send("p_y3", block(3, 0), block(3, 1), peer(dyh=1))
            await_("p_z5", block(5, 0))
            send("p_z4b", block(5, 0, 1), block(4, 0, 1), peer(dz=1))
            send("p_y5", block(5, 0), block(5, 1), peer(dyh=1))
            await_("p_y2", block(2, 1))
        elif g == 6:
            await_("p_y6", block(6, 1))
        elif g == 3:
            await_("p_z4a", block(4, 0, 0))
            send("p_y4a", block(4, 0, 0), block(4, 1, 0), peer(dyh=1))
            await_("p_z4b", block(4, 0, 1))
            send("p_y4b", block(4, 0, 1), block(4, 1, 1), peer(dyh=1))
            await_("p_y3", block(3, 1))
        elif g == 5:
            await_("p_y5", block(5, 1))
        elif g == 4:
            await_("p_y4a", block(4, 1, 0))
            await_("p_y4b", block(4, 1, 1))

    def pass_one(g, slot, before, before_slot, before_peak):
        def body(i, carry):
            rows = pl.ds(pl.multiple_of(i * KC, KC), KC)
            peak, total = carry
            if g is not None:
                inner = lax.dot_general(
                    narrow[rows, :], pbuf[g], (((1,), (1,)), ((), ())), preferred_element_type=F32
                )
                half = norm[rows, :]
                inner = inner - jnp.concatenate([half, half], axis=1)
                scores[slot, rows, :] = inner
                peak = jnp.maximum(peak, jnp.max(inner.reshape(KC // 8, 8, GR), axis=0))
            if before is not None:
                shifted = scores[before_slot, rows, :].reshape(KC // 8, 8, GR) - before_peak[None]
                weight = jnp.exp2(shifted * C2)
                total = total + jnp.sum(weight, axis=0)
                ebuf[rows, before * GR : (before + 1) * GR] = weight.reshape(KC, GR).astype(BF)
            return peak, total

        start = (jnp.full((8, GR), -jnp.inf, F32), jnp.zeros((8, GR), F32))
        return lax.fori_loop(0, K // KC, body, start)

    before, before_peak = None, None
    for n, g in enumerate(ORDER + (None,)):
        if g is not None:
            arrive(g)
        peak, total = pass_one(g, n % 2, before, (n + 1) % 2, before_peak)
        if before is not None:
            row_peak = before_peak[0:1]
            row_lse = SHARP * row_peak + jnp.log(jnp.sum(total, axis=0, keepdims=True))
            plane = ((z + before) % 8) * 2
            peaks[2 * before : 2 * before + 1, :] = row_peak[:, 0:RB]
            peaks[2 * before + 1 : 2 * before + 2, :] = row_peak[:, RB:GR]
            mine[pl.ds(plane + yhi, 1), :] = row_lse[:, 0:RB]
            mine[pl.ds(plane + 1 - yhi, 1), :] = row_lse[:, RB:GR]
        if g is not None:
            before, before_peak = g, jnp.broadcast_to(jnp.max(peak, axis=0, keepdims=True), (8, GR))

    for a in range(8):
        for b in range(2):
            if a or b:
                send(f"s_{a}{b}", mine, stats.at[2 * a + b], peer(dz=a, dyh=b))
    stats[0] = mine[...]
    for a in range(8):
        for b in range(2):
            if a or b:
                await_(f"s_{a}{b}", stats.at[2 * a + b])
    every = stats[...]
    top = jnp.max(every, axis=0)
    lse_abs[...] = top + jnp.log(jnp.sum(jnp.exp(every - top[None]), axis=0))
    lse_out[...] = lse_abs[pl.ds(shard, 1), :]
    fpad[...] = jnp.zeros((128, 128), F32)
    for j in range(16):
        row = ((z + j // 2) % 8) * 2 + (yhi + j % 2) % 2
        fpad[j : j + 1, :] = jnp.exp(SHARP * peaks[j : j + 1, :] - lse_abs[pl.ds(row, 1), :])
    factor = fpad[...]
    column = jnp.transpose(factor)
    line = lax.broadcasted_iota(jnp.int32, (16, 128), 0)
    for j in range(16):
        rows = pbuf[j // 2, (j % 2) * RB : (j % 2 + 1) * RB, :].astype(F32)
        pf[j * RB : (j + 1) * RB, :] = (rows * column[:, j : j + 1]).astype(BF)
        value = jnp.broadcast_to(factor[j : j + 1, :], (16, 128))
        high = value.astype(BF).astype(F32)
        fl[:, j * RB : (j + 1) * RB] = jnp.where(
            line == 0, high, jnp.where(line == 1, value - high, 0.0)
        ).astype(BF)

    mine_at = pl.ds(pl.multiple_of(core * CH, CH), CH)
    sib_at = pl.ds(pl.multiple_of((1 - core) * CH, CH), CH)
    line2 = lax.broadcasted_iota(jnp.int32, (16, CH), 0)

    def first(dyl, dx):
        return (((ylo + dyl) % 2) * 4 + (x + dx) % 4) * (2 * CH)

    def weigh(dyl, dx):
        s = dyl * 4 + dx
        base = first(dyl, dx)
        part[s] = jnp.dot(
            ebuf[pl.ds(pl.multiple_of(base, 2 * CH), 2 * CH), :], pf[...], preferred_element_type=F32
        )
        for which, dst in ((core, mpart), (1 - core, hmass)):
            rows = pl.ds(pl.multiple_of(base + which * CH, CH), CH)
            mass = lax.dot_general(
                fl[...], ebuf[rows, :], (((1,), (1,)), ((), ())), preferred_element_type=F32
            )
            dst[s] = jnp.broadcast_to(mass[0:1] + mass[1:2], (8, CH))
        send(f"h_{dyl}{dx}", part.at[s, sib_at], hpart.at[s], peer(dc=1))
        send(f"n_{dyl}{dx}", hmass.at[s], nmass.at[s], peer(dc=1))

    def local(dyl, dx):
        s = dyl * 4 + dx
        await_(f"h_{dyl}{dx}", hpart.at[s])
        await_(f"n_{dyl}{dx}", nmass.at[s])
        return part[s, mine_at, :] + hpart[s], mpart[s, 0:1, :] + nmass[s, 0:1, :]

    def put(s, total, mass, split=False):
        high = mass.astype(BF).astype(F32)
        extra = jnp.where(line2 == 0, high, jnp.where(line2 == 1, mass - high, 0.0)).astype(BF)
        coded = encode(total).astype(BF)
        if split:
            message[s, 0:128, :] = coded[0:128]
            message[s, 128:144, :] = extra
            message[s, 144:272, :] = coded[128:256]
        else:
            message[s, 0:256, :] = coded
            message[s, 256:272, :] = extra

    def masses_in(rows):
        rows = rows.astype(F32)
        return rows[0:1] + rows[1:2]

    def got(name, s):
        await_(name, inbox.at[s])
        return decode(inbox[s, 0:256, :].astype(F32)), masses_in(inbox[s, 256:272, :])

    weigh(1, 2)
    weigh(1, 1)
    put(0, *local(1, 2))
    send("r_12", message.at[0], inbox.at[0], peer(dyl=1))
    weigh(1, 3)
    put(1, *local(1, 1))
    send("r_11", message.at[1], inbox.at[1], peer(dx=1))
    weigh(0, 2)
    put(2, *local(1, 3))
    send("r_13", message.at[2], inbox.at[2], peer(dx=-1))
    weigh(1, 0)
    total, mass = local(0, 2)
    other, other_mass = got("r_12", 0)
    put(3, total + other, mass + other_mass, split=True)
    send("r_a", message.at[3, pl.ds(0, 144)], inbox.at[3, pl.ds(0, 144)], peer(dx=1))
    send("r_b", message.at[3, pl.ds(144, 128)], inbox.at[3, pl.ds(144, 128)], peer(dx=-1))
    weigh(0, 1)
    total, mass = local(1, 0)
    for name, s in (("r_11", 1), ("r_13", 2)):
        other, other_mass = got(name, s)
        total, mass = total + other, mass + other_mass
    put(4, total, mass)
    send("r_y", message.at[4], inbox.at[4], peer(dyl=1))
    weigh(0, 3)
    weigh(0, 0)
    total, mass = local(0, 1)
    await_("r_a", inbox.at[3, pl.ds(0, 144)])
    total = jnp.concatenate([total[0:128] + decode(inbox[3, 0:128, :].astype(F32)), total[128:256]], axis=0)
    put(5, total, mass + masses_in(inbox[3, 128:144, :]))
    send("r_p", message.at[5], inbox.at[5], peer(dx=1))
    total, mass = local(0, 3)
    await_("r_b", inbox.at[3, pl.ds(144, 128)])
    total = jnp.concatenate([total[0:128], total[128:256] + decode(inbox[3, 144:272, :].astype(F32))], axis=0)
    put(6, total, mass)
    send("r_m", message.at[6], inbox.at[6], peer(dx=-1))
    total, mass = local(0, 0)
    for name, s in (("r_y", 4), ("r_p", 5), ("r_m", 6)):
        other, other_mass = got(name, s)
        total, mass = total + other, mass + other_mass

    def owned(dyl, dx, half=None, dc=0):
        start = first(dyl, dx) + ((core + dc) % 2) * CH
        if half is None:
            return out.at[pl.ds(pl.multiple_of(start, CH), CH)]
        return out.at[pl.ds(pl.multiple_of(start + half * (CH // 2), CH // 2), CH // 2)]

    own_at = pl.ds(pl.multiple_of(first(0, 0) + core * CH, CH), CH)
    wide = jnp.transpose(jnp.broadcast_to(mass, (128, CH))) + 1.0
    updated = (total + cb[own_at, :]) / jnp.concatenate([wide, wide], axis=1)
    out[own_at, :] = encode(updated).astype(BF)

    send("g_y", owned(0, 0), owned(0, 0), peer(dyl=1))
    send("g_p", owned(0, 0), owned(0, 0), peer(dx=1))
    send("g_m", owned(0, 0), owned(0, 0), peer(dx=-1))
    send("t_00", owned(0, 0), owned(0, 0), peer(dc=1))

    def relay(name, ref, sibling, *further):
        await_(name, ref)
        for target, device, piece in further:
            send(target, piece, piece, device)
        send(sibling, ref, ref, peer(dc=1))

    relay("g_y", owned(1, 0), "t_10", ("g_11", peer(dx=-1), owned(1, 0)), ("g_13", peer(dx=1), owned(1, 0)))
    relay("g_m", owned(0, 1), "t_01", ("g_a", peer(dx=-1), owned(0, 1, 0)))
    relay("g_p", owned(0, 3), "t_03", ("g_b", peer(dx=1), owned(0, 3, 1)))
    relay("g_a", owned(0, 2, 0), "t_2a", ("g_ya", peer(dyl=1), owned(0, 2, 0)))
    relay("g_b", owned(0, 2, 1), "t_2b", ("g_yb", peer(dyl=1), owned(0, 2, 1)))
    relay("g_11", owned(1, 1), "t_11")
    relay("g_13", owned(1, 3), "t_13")
    relay("g_ya", owned(1, 2, 0), "t_12a")
    relay("g_yb", owned(1, 2, 1), "t_12b")
    for name, ref in (
        ("t_00", owned(0, 0, dc=1)), ("t_10", owned(1, 0, dc=1)), ("t_01", owned(0, 1, dc=1)),
        ("t_03", owned(0, 3, dc=1)), ("t_2a", owned(0, 2, 0, dc=1)), ("t_2b", owned(0, 2, 1, dc=1)),
        ("t_11", owned(1, 1, dc=1)), ("t_13", owned(1, 3, dc=1)), ("t_12a", owned(1, 2, 0, dc=1)),
        ("t_12b", owned(1, 2, 1, dc=1)),
    ):
        await_(name, ref)
    for one in sent.values():
        one.wait_send()


def shards(points, codebook):
    n = len(NAMES)
    coded, lse = pl.pallas_call(
        kernel,
        out_shape=(jax.ShapeDtypeStruct((K, W), BF), jax.ShapeDtypeStruct((1, RB), F32)),
        in_specs=[pl.BlockSpec(memory_space=pltpu.VMEM), pl.BlockSpec(memory_space=pl.ANY)],
        out_specs=[pl.BlockSpec(memory_space=pltpu.VMEM)] * 2,
        scratch_shapes=[
            pltpu.VMEM((K, W), F32),
            pltpu.VMEM((K, W), BF),
            pltpu.VMEM((K, 128), F32),
            pltpu.VMEM((8, GR, W), BF),
            pltpu.VMEM((R, W), BF),
            pltpu.VMEM((16, R), BF),
            pltpu.VMEM((2, K, GR), F32),
            pltpu.VMEM((K, R), BF),
            pltpu.VMEM((16, RB), F32),
            pltpu.VMEM((16, RB), F32),
            pltpu.VMEM((16, 16, RB), F32),
            pltpu.VMEM((16, RB), F32),
            pltpu.VMEM((128, 128), F32),
            pltpu.VMEM((8, 2 * CH, W), F32),
            pltpu.VMEM((8, CH, W), F32),
            pltpu.VMEM((8, 8, CH), F32),
            pltpu.VMEM((8, 8, CH), F32),
            pltpu.VMEM((8, 8, CH), F32),
            pltpu.VMEM((7, CH + 16, W), BF),
            pltpu.VMEM((7, CH + 16, W), BF),
            pltpu.SemaphoreType.DMA((4,)),
            pltpu.SemaphoreType.DMA((n,)),
            pltpu.SemaphoreType.DMA((n,)),
        ],
        compiler_params=pltpu.CompilerParams(
            collective_id=0, has_side_effects=True, vmem_limit_bytes=60 << 20
        ),
        cost_estimate=pl.CostEstimate(flops=4 * R * K * W, bytes_accessed=8 << 20, transcendentals=R * K),
    )(points, codebook)
    return decode(coded.astype(F32)), lse.reshape(RB)


def solution(mesh):
    in_specs = (P(("dp", "shard"), None), P("shard", None))
    out_specs = (P("shard", None), P(("dp", "shard")))
    return jax.shard_map(shards, mesh=mesh, in_specs=in_specs, out_specs=out_specs, check_vma=False)
```

time: 435 us -> 86.3 us (0.20)
  waiting for transfers between devices: 161 us -> 0 us
  blocking collectives: 131 us -> 0 us
  Pallas kernels: 0 us -> 80 us
  matrix products: 64.9 us -> 0 us
  other arithmetic: 62.3 us -> 4.96 us
  between operations: 14.2 us -> 0.65 us
    psum x2 -> x0, blocking collectives: 99.1 us -> none  [the longest x1 67.1 us: shards(): total_sums, total_masses = lax.psum((centroid_sums, masses), 'dp')]
    psum x1 -> x0, waiting for transfers between devices: 82.9 us -> none  [shards(): total_sums, total_masses = lax.psum((centroid_sums, masses), 'dp')]
    pallas_call x0 -> x1, Pallas kernels: none -> 80 us  [shards(): pl.pallas_call(kernel, out_shape=(jax.ShapeDtypeStruct((K, W), BF), jax.S...]
    all_gather x1 -> x0, waiting for transfers between devices: 77.2 us -> none  [shards(): gathered = lax.all_gather(points, 'shard', axis=0, tiled=True)]
    dot_general x8 -> x0, matrix products: 64.9 us -> none  [the longest x4 33 us: advance(): lax.dot_general(assigned, block_rows, (((0,), (0,)), ((), ())), preferred...]
    reduce_sum x9 -> x0, other arithmetic: 41.8 us -> none  [the longest x4 19 us: advance(): masses = masses + jnp.sum(assigned.astype(jnp.float32), axis=0)]
    pmax x1 -> x0, blocking collectives: 31.6 us -> none  [shards(): global_peak = lax.pmax(row_peaks, 'shard')]
    reduce_max x4 -> x0, other arithmetic: 15.4 us -> none  [local_stats(): row_peak = jnp.max(scores, axis=1)]
  transfers between devices with their start and end apart: 2 -> 0, of which waited for: 2 -> 0; matrix products, arithmetic and copies ran while one was open for 1% -> 0% of each run, Pallas kernels for 0% -> 0%
where the time goes in v1:
time: 86.3 us; the launch traced here: 86.1 us
  Pallas kernels  80 us (93%)
  other arithmetic  4.96 us (6%)
    pallas_call x1, Pallas kernels, shards(): pl.pallas_call(kernel, out_shape=(jax.ShapeDtypeStruct((K, W), BF), jax.S...  80 us
    select_n x1, other arithmetic, decode(): return jnp.where(power < 0.0, -root, root)  4.96 us

profile of v1, /device:TPU:1, one launch (start us, length us, event | category | flops | bytes accessed | tf_op | source)
XLA Modules:
  0.0 86.1 jit_solution(17450790803671771347)
XLA Ops:
  0.6 80.0 %shard_map.41 = (bf16[4096,256]{1,0:T(8,128)(2,1)}, f32[1,128]{1,0:T(1,128)}) custom-call(bf16[128,256]{1,0:T(8,128)(2,1)} %points.1, f32[4096,256]{1,0:T(8,128)} %codebook.1), custom_call_target="tpu_custom_call" | custom-call | flops 8589934592 | bytes 8388608 | tf_op jit(solution)/shard_map/pallas_call | solution.py:357
  80.7 0.0 copy-start
  80.7 5.0 %negate_select_fusion = f32[4096,256]{1,0:T(8,128)} fusion(bf16[4096,256]{1,0:T(8,128)(2,1)} %get-tuple-element.4), kind=kLoop, calls=%fused_computation | loop fusion | flops 8388608 | bytes 6291456 | tf_op jit(solution)/shard_map/jit(_where)/select_n | solution.py:46
  85.6 0.0 copy-done
  85.6 0.5 copy.5
Async XLA Ops:
  80.7 5.0 %copy-start = (f32[1,128]{1,0:T(1,128)S(1)}, f32[1,128]{1,0:T(1,128)}, u32[]{:S(2)}) copy-start(f32[1,128]{1,0:T(1,128)} %get-tuple-element.5) | copy-start | bytes 1540

commit v2 on v1

v2 whole, which is shorter than its diff:
```python
import math

import jax
import jax.numpy as jnp
from jax import lax
from jax.experimental import pallas as pl
from jax.experimental.pallas import tpu as pltpu
from jax.sharding import PartitionSpec as P

MESH = pl.DeviceIdType.MESH
BF = jnp.bfloat16
F32 = jnp.float32
W = 256
K = 4096
RB = 128
GR = 2 * RB
R = 16 * RB
CH = 256
Q = 4
QR = CH // Q
SHARP = 4.0 / math.sqrt(W)
C2 = SHARP / math.log(2.0)

NAMES = (
    ["p_y0", "p_z1", "p_z7", "p_z2", "p_z6", "p_z3", "p_z5", "p_z4a", "p_z4b", "p_q1", "p_q7"]
    + ["p_y2", "p_y6", "p_y3", "p_y5", "p_y4a", "p_y4b"]
    + [f"s_{a}{b}" for a in range(8) for b in range(2) if a or b]
    + [f"h_{a}{b}" for a in range(2) for b in range(4)]
    + [f"n_{a}{b}" for a in range(2) for b in range(4)]
    + [f"r_{a}{q}" for a in ("12", "11", "13", "02", "y", "p", "m") for q in range(Q)]
    + [f"g_{a}{q}" for a in ("p", "m", "y", "2", "11", "13", "y2") for q in range(Q)]
    + [f"t_{a}{b}{q}" for a in range(2) for b in range(4) for q in range(Q)]
)
INDEX = {name: i for i, name in enumerate(NAMES)}
ORDER = (0, 1, 7, 2, 6, 3, 5, 4)


def encode(value):
    return (value * jnp.abs(value)) * (value * value)


def decode(power):
    size = jnp.abs(power)
    root = lax.rsqrt(lax.rsqrt(jnp.maximum(size, 1e-37)))
    root = jnp.where(size < 1e-37, 0.0, root)
    return jnp.where(power < 0.0, -root, root)


def kernel(
    points, codebook, out, lse_out,
    cb, narrow, norm, pbuf, pf, scores, ebuf, peaks, mine, stats, lse_abs, fpad, part, hpart, mpart,
    nmass, message, inbox, cb_sem, send_sem, recv_sem,
):
    dp, shard = lax.axis_index("dp"), lax.axis_index("shard")
    ylo, x, core = dp // 8, (dp // 2) % 4, dp % 2
    z, yhi = shard // 2, shard % 2

    def peer(dyl=0, dx=0, dc=0, dz=0, dyh=0):
        return {
            "dp": ((ylo + dyl) % 2) * 8 + ((x + dx + 4) % 4) * 2 + (core + dc) % 2,
            "shard": ((z + dz + 8) % 8) * 2 + (yhi + dyh) % 2,
        }

    barrier = pltpu.get_barrier_semaphore()
    others = [peer(dz=a) for a in (-2, -1, 1, 2)] + [peer(dyh=1)]
    others += [peer(dx=1), peer(dx=-1), peer(dyl=1), peer(dc=1)]
    for other in others:
        pl.semaphore_signal(barrier, inc=1, device_id=other, device_id_type=MESH)

    loads = []
    for i in range(4):
        rows = pl.ds(i * (K // 4), K // 4)
        loads.append(pltpu.make_async_copy(codebook.at[rows], cb.at[rows], cb_sem.at[i]))
        loads[-1].start()
    pbuf[0, 0:RB, :] = points[...]
    for i in range(4):
        loads[i].wait()

        def prepare(j, unused, i=i):
            rows = pl.ds(pl.multiple_of(i * (K // 4) + j * 256, 256), 256)
            value = cb[rows, :]
            narrow[rows, :] = value.astype(BF)
            half = 0.5 * jnp.sum(value * value, axis=1, keepdims=True)
            norm[rows, :] = jnp.broadcast_to(half, (256, 128))
            return unused

        lax.fori_loop(0, K // 4 // 256, prepare, 0)

    pl.semaphore_wait(barrier, len(others))

    sent = {}

    def copy(name, src, dst, device):
        i = INDEX[name]
        return pltpu.make_async_remote_copy(
            src_ref=src, dst_ref=dst, send_sem=send_sem.at[i], recv_sem=recv_sem.at[i],
            device_id=device, device_id_type=MESH,
        )

    def send(name, src, dst, device):
        sent[name] = copy(name, src, dst, device)
        sent[name].start()

    def await_(name, dst):
        copy(name, dst, dst, peer(dc=1)).wait_recv()

    def block(dz, dy, half=None):
        if half is None:
            return pbuf.at[dz % 8, pl.ds(dy * RB, RB)]
        return pbuf.at[dz % 8, pl.ds(dy * RB + half * (RB // 2), RB // 2)]

    own = block(0, 0)
    send("p_y0", own, block(0, 1), peer(dyh=1))
    send("p_z1", own, block(1, 0), peer(dz=-1))
    send("p_z7", own, block(7, 0), peer(dz=1))
    send("p_z2", own, block(2, 0), peer(dz=-2))
    send("p_z6", own, block(6, 0), peer(dz=2))

    def arrive(g):
        if g == 0:
            await_("p_y0", block(0, 1))
            send("p_q1", block(0, 1), block(1, 1), peer(dz=-1))
            send("p_q7", block(0, 1), block(7, 1), peer(dz=1))
        elif g == 1:
            await_("p_z1", block(1, 0))
            await_("p_z7", block(7, 0))
            await_("p_z2", block(2, 0))
            send("p_z3", block(2, 0), block(3, 0), peer(dz=-1))
            send("p_y2", block(2, 0), block(2, 1), peer(dyh=1))
            await_("p_z6", block(6, 0))
            send("p_z5", block(6, 0), block(5, 0), peer(dz=1))
            send("p_y6", block(6, 0), block(6, 1), peer(dyh=1))
            await_("p_q1", block(1, 1))
        elif g == 7:
            await_("p_q7", block(7, 1))
        elif g == 2:
            await_("p_z3", block(3, 0))
            send("p_z4a", block(3, 0, 0), block(4, 0, 0), peer(dz=-1))
            send("p_y3", block(3, 0), block(3, 1), peer(dyh=1))
            await_("p_z5", block(5, 0))
            send("p_z4b", block(5, 0, 1), block(4, 0, 1), peer(dz=1))
            send("p_y5", block(5, 0), block(5, 1), peer(dyh=1))
            await_("p_y2", block(2, 1))
        elif g == 6:
            await_("p_y6", block(6, 1))
        elif g == 3:
            await_("p_z4a", block(4, 0, 0))
            send("p_y4a", block(4, 0, 0), block(4, 1, 0), peer(dyh=1))
            await_("p_z4b", block(4, 0, 1))
            send("p_y4b", block(4, 0, 1), block(4, 1, 1), peer(dyh=1))
            await_("p_y3", block(3, 1))
        elif g == 5:
            await_("p_y5", block(5, 1))
        elif g == 4:
            await_("p_y4a", block(4, 1, 0))
            await_("p_y4b", block(4, 1, 1))

    def pass_one(g, slot, before, before_slot, before_peak):
        peak, total = jnp.full((8, GR), -jnp.inf, F32), None
        if g is not None:
            inner = lax.dot_general(
                narrow[...], pbuf[g], (((1,), (1,)), ((), ())), preferred_element_type=F32
            )
            half = norm[...]
            inner = inner - jnp.concatenate([half, half], axis=1)
            scores[slot] = inner
            peak = jnp.max(inner.reshape(K // 8, 8, GR), axis=0)
        if before is not None:
            shifted = scores[before_slot].reshape(K // 8, 8, GR) - before_peak[None]
            weight = jnp.exp2(shifted * C2)
            total = jnp.sum(weight, axis=0)
            ebuf[:, before * GR : (before + 1) * GR] = weight.reshape(K, GR).astype(BF)
        return peak, total

    before, before_peak = None, None
    for n, g in enumerate(ORDER + (None,)):
        if g is not None:
            arrive(g)
        peak, total = pass_one(g, n % 2, before, (n + 1) % 2, before_peak)
        if before is not None:
            row_peak = before_peak[0:1]
            row_lse = SHARP * row_peak + jnp.log(jnp.sum(total, axis=0, keepdims=True))
            plane = ((z + before) % 8) * 2
            peaks[2 * before : 2 * before + 1, :] = row_peak[:, 0:RB]
            peaks[2 * before + 1 : 2 * before + 2, :] = row_peak[:, RB:GR]
            mine[pl.ds(plane + yhi, 1), :] = row_lse[:, 0:RB]
            mine[pl.ds(plane + 1 - yhi, 1), :] = row_lse[:, RB:GR]
        if g is not None:
            before, before_peak = g, jnp.broadcast_to(jnp.max(peak, axis=0, keepdims=True), (8, GR))

    for a in range(8):
        for b in range(2):
            if a or b:
                send(f"s_{a}{b}", mine, stats.at[2 * a + b], peer(dz=a, dyh=b))
    stats[0] = mine[...]
    for a in range(8):
        for b in range(2):
            if a or b:
                await_(f"s_{a}{b}", stats.at[2 * a + b])
    every = stats[...]
    top = jnp.max(every, axis=0)
    lse_abs[...] = top + jnp.log(jnp.sum(jnp.exp(every - top[None]), axis=0))
    lse_out[...] = lse_abs[pl.ds(shard, 1), :]
    fpad[...] = jnp.zeros((128, 128), F32)
    for j in range(16):
        row = ((z + j // 2) % 8) * 2 + (yhi + j % 2) % 2
        fpad[j : j + 1, :] = jnp.exp(SHARP * peaks[j : j + 1, :] - lse_abs[pl.ds(row, 1), :])
    factor = fpad[...]
    column = jnp.transpose(factor)
    for j in range(16):
        rows = pbuf[j // 2, (j % 2) * RB : (j % 2 + 1) * RB, :].astype(F32)
        pf[j * RB : (j + 1) * RB, :] = (rows * column[:, j : j + 1]).astype(BF)

    mine_at = pl.ds(pl.multiple_of(core * CH, CH), CH)
    sib_at = pl.ds(pl.multiple_of((1 - core) * CH, CH), CH)
    line = lax.broadcasted_iota(jnp.int32, (16, CH), 0)

    def first(dyl, dx):
        return (((ylo + dyl) % 2) * 4 + (x + dx) % 4) * (2 * CH)

    def weigh(dyl, dx):
        s = dyl * 4 + dx
        rows = pl.ds(pl.multiple_of(first(dyl, dx), 2 * CH), 2 * CH)
        weights = ebuf[rows, :]
        part[s] = jnp.dot(weights, pf[...], preferred_element_type=F32)
        lanes = jnp.zeros((2 * CH, RB), F32)
        for j in range(16):
            lanes = lanes + weights[:, j * RB : (j + 1) * RB].astype(F32) * fpad[j : j + 1, :]
        for j in range(2 * CH // 128):
            mass = jnp.sum(jnp.transpose(lanes[j * 128 : (j + 1) * 128, :]), axis=0, keepdims=True)
            mpart[s, j // 2, :, (j % 2) * 128 : (j % 2 + 1) * 128] = jnp.broadcast_to(mass, (8, 128))
        send(f"h_{dyl}{dx}", part.at[s, sib_at], hpart.at[s], peer(dc=1))
        send(f"n_{dyl}{dx}", mpart.at[s, 1 - core], nmass.at[s], peer(dc=1))

    def local(dyl, dx):
        s = dyl * 4 + dx
        await_(f"h_{dyl}{dx}", hpart.at[s])
        await_(f"n_{dyl}{dx}", nmass.at[s])
        part[s, mine_at, :] = part[s, mine_at, :] + hpart[s]
        return mpart[s, core, 0:1, :] + nmass[s, 0:1, :]

    def piece(dyl, dx, q):
        return part[dyl * 4 + dx, pl.ds(pl.multiple_of(core * CH + q * QR, QR), QR), :]

    def slot(ref, s, q):
        return ref.at[s, pl.ds(0, 16 + QR)] if q == 0 else ref.at[s, pl.ds(16 + q * QR, QR)]

    def put(kind, s, q, total, mass, device):
        if q == 0:
            high = mass.astype(BF).astype(F32)
            message[s, 0:16, :] = jnp.where(
                line == 0, high, jnp.where(line == 1, mass - high, 0.0)
            ).astype(BF)
        message[s, 16 + q * QR : 16 + (q + 1) * QR, :] = encode(total).astype(BF)
        send(f"r_{kind}{q}", slot(message, s, q), slot(inbox, s, q), device)

    def got(kind, s, q):
        await_(f"r_{kind}{q}", slot(inbox, s, q))
        return decode(inbox[s, 16 + q * QR : 16 + (q + 1) * QR, :].astype(F32))

    def got_mass(s):
        rows = inbox[s, 0:16, :].astype(F32)
        return rows[0:1] + rows[1:2]

    weigh(1, 2)
    weigh(1, 1)
    mass = local(1, 2)
    for q in range(Q):
        put("12", 0, q, piece(1, 2, q), mass, peer(dyl=1))
    weigh(1, 3)
    mass = local(1, 1)
    for q in range(Q):
        put("11", 1, q, piece(1, 1, q), mass, peer(dx=1))
    weigh(0, 2)
    mass = local(1, 3)
    for q in range(Q):
        put("13", 2, q, piece(1, 3, q), mass, peer(dx=-1))
    weigh(0, 1)
    mass = local(0, 2)
    for q in (0, 2, 1, 3):
        total = piece(0, 2, q) + got("12", 0, q)
        if q == 0:
            mass = mass + got_mass(0)
        put("02", 3, q, total, mass, peer(dx=1 if q < Q // 2 else -1))
    weigh(0, 3)
    mass_p = local(0, 1)
    for q in range(Q // 2, Q):
        put("p", 5, q, piece(0, 1, q), mass_p, peer(dx=1))
    weigh(1, 0)
    mass_m = local(0, 3)
    for q in range(Q // 2):
        put("m", 6, q, piece(0, 3, q), mass_m, peer(dx=-1))
    weigh(0, 0)
    mass = local(1, 0)
    for q in range(Q):
        total = piece(1, 0, q) + got("11", 1, q) + got("13", 2, q)
        if q == 0:
            mass = mass + got_mass(1) + got_mass(2)
        put("y", 4, q, total, mass, peer(dyl=1))
        if q < Q // 2:
            total = piece(0, 1, q) + got("02", 3, q)
            if q == 0:
                mass_p = mass_p + got_mass(3)
            put("p", 5, q, total, mass_p, peer(dx=1))
            late = q + Q // 2
            put("m", 6, late, piece(0, 3, late) + got("02", 3, late), mass_m, peer(dx=-1))
    mass = local(0, 0)

    def owned(dyl, dx, q, dc=0):
        start = first(dyl, dx) + ((core + dc) % 2) * CH + q * QR
        return out.at[pl.ds(pl.multiple_of(start, QR), QR)]

    def spread(name, dyl, dx, q, *further):
        ref = owned(dyl, dx, q)
        if name is not None:
            await_(f"g_{name}{q}", ref)
        for target, device in further:
            send(f"g_{target}{q}", ref, ref, device)
        send(f"t_{dyl}{dx}{q}", ref, ref, peer(dc=1))

    wide = None
    for q in range(Q):
        total = piece(0, 0, q) + got("y", 4, q)
        if q < Q // 2:
            total = total + got("m", 6, q) + got("p", 5, q)
        else:
            total = total + got("p", 5, q) + got("m", 6, q)
        if q == 0:
            mass = mass + got_mass(4) + got_mass(5) + got_mass(6)
            wide = jnp.transpose(jnp.broadcast_to(mass, (128, CH))) + 1.0
        own_at = pl.ds(pl.multiple_of(first(0, 0) + core * CH + q * QR, QR), QR)
        below = wide[q * QR : (q + 1) * QR, :]
        updated = (total + cb[own_at, :]) / jnp.concatenate([below, below], axis=1)
        out[own_at, :] = encode(updated).astype(BF)
        spread(None, 0, 0, q, ("y", peer(dyl=1)), ("p", peer(dx=1)), ("m", peer(dx=-1)))
    for q in range(Q):
        spread("y", 1, 0, q, ("11", peer(dx=-1)), ("13", peer(dx=1)))
        spread("m", 0, 1, q, *([("2", peer(dx=-1))] if q < Q // 2 else []))
        spread("p", 0, 3, q, *([("2", peer(dx=1))] if q >= Q // 2 else []))
    for q in range(Q):
        spread("2", 0, 2, q, ("y2", peer(dyl=1)))
        spread("11", 1, 1, q)
        spread("13", 1, 3, q)
    for q in range(Q):
        spread("y2", 1, 2, q)
    for a in range(2):
        for b in range(4):
            for q in range(Q):
                await_(f"t_{a}{b}{q}", owned(a, b, q, dc=1))
    for one in sent.values():
        one.wait_send()


def decode_kernel(coded, updated):
    updated[...] = decode(coded[...].astype(F32))


def shards(points, codebook):
    n = len(NAMES)
    coded, lse = pl.pallas_call(
        kernel,
        out_shape=(jax.ShapeDtypeStruct((K, W), BF), jax.ShapeDtypeStruct((1, RB), F32)),
        in_specs=[pl.BlockSpec(memory_space=pltpu.VMEM), pl.BlockSpec(memory_space=pl.ANY)],
        out_specs=[pl.BlockSpec(memory_space=pltpu.VMEM)] * 2,
        scratch_shapes=[
            pltpu.VMEM((K, W), F32),
            pltpu.VMEM((K, W), BF),
            pltpu.VMEM((K, 128), F32),
            pltpu.VMEM((8, GR, W), BF),
            pltpu.VMEM((R, W), BF),
            pltpu.VMEM((2, K, GR), F32),
            pltpu.VMEM((K, R), BF),
            pltpu.VMEM((16, RB), F32),
            pltpu.VMEM((16, RB), F32),
            pltpu.VMEM((16, 16, RB), F32),
            pltpu.VMEM((16, RB), F32),
            pltpu.VMEM((128, 128), F32),
            pltpu.VMEM((8, 2 * CH, W), F32),
            pltpu.VMEM((8, CH, W), F32),
            pltpu.VMEM((8, 2, 8, CH), F32),
            pltpu.VMEM((8, 8, CH), F32),
            pltpu.VMEM((7, CH + 16, W), BF),
            pltpu.VMEM((7, CH + 16, W), BF),
            pltpu.SemaphoreType.DMA((4,)),
            pltpu.SemaphoreType.DMA((n,)),
            pltpu.SemaphoreType.DMA((n,)),
        ],
        compiler_params=pltpu.CompilerParams(
            collective_id=0, has_side_effects=True, vmem_limit_bytes=60 << 20
        ),
        cost_estimate=pl.CostEstimate(flops=4 * R * K * W, bytes_accessed=8 << 20, transcendentals=R * K),
    )(points, codebook)
    rows = K // 4
    updated = pl.pallas_call(
        decode_kernel,
        out_shape=jax.ShapeDtypeStruct((K, W), F32),
        grid=(4,),
        in_specs=[pl.BlockSpec((rows, W), lambda i: (i, 0))],
        out_specs=pl.BlockSpec((rows, W), lambda i: (i, 0)),
    )(coded)
    return updated, lse.reshape(RB)


def solution(mesh):
    in_specs = (P(("dp", "shard"), None), P("shard", None))
    out_specs = (P("shard", None), P(("dp", "shard")))
    return jax.shard_map(shards, mesh=mesh, in_specs=in_specs, out_specs=out_specs, check_vma=False)
```

time: 86.3 us -> 81.5 us (0.944)
  other arithmetic: 4.96 us -> 0 us
    select_n x1 -> x0, other arithmetic: 4.96 us -> none  [decode(): return jnp.where(power < 0.0, -root, root)]
    pallas_call x0 -> x1, Pallas kernels: none -> 4.76 us  [shards(): pl.pallas_call(decode_kernel, out_shape=jax.ShapeDtypeStruct((K, W), F32)...]
    pallas_call x1, Pallas kernels: 80 us -> 75.4 us  [shards(): pl.pallas_call(kernel, out_shape=(jax.ShapeDtypeStruct((K, W), BF), jax.S...]
where the time goes in v2:
time: 81.5 us; the launch traced here: 81.3 us
  Pallas kernels  80.1 us (98%)
    pallas_call x1, Pallas kernels, shards(): pl.pallas_call(kernel, out_shape=(jax.ShapeDtypeStruct((K, W), BF), jax.S...  75.4 us
    pallas_call x1, Pallas kernels, shards(): pl.pallas_call(decode_kernel, out_shape=jax.ShapeDtypeStruct((K, W), F32)...  4.76 us

profile of v2, /device:TPU:1, one launch (start us, length us, event | category | flops | bytes accessed | tf_op | source)
XLA Modules:
  0.0 81.3 jit_solution(8766114416438039848)
XLA Ops:
  0.6 75.4 %shard_map.41 = (bf16[4096,256]{1,0:T(8,128)(2,1)}, f32[1,128]{1,0:T(1,128)}) custom-call(bf16[128,256]{1,0:T(8,128)(2,1)} %points.1, f32[4096,256]{1,0:T(8,128)} %codebook.1), custom_call_target="tpu_custom_call" | custom-call | flops 8589934592 | bytes 8388608 | tf_op jit(solution)/shard_map/pallas_call | solution.py:360
  76.0 0.0 copy-start
  76.0 4.8 %shard_map.42 = f32[4096,256]{1,0:T(8,128)} custom-call(bf16[4096,256]{1,0:T(8,128)(2,1)} %get-tuple-element.4.coded), custom_call_target="tpu_custom_call" | custom-call | tf_op jit(solution)/shard_map/pallas_call | solution.py:394
  80.8 0.0 copy-done
  80.8 0.5 copy.5
Async XLA Ops:
  76.0 4.8 %copy-start = (f32[1,128]{1,0:T(1,128)S(1)}, f32[1,128]{1,0:T(1,128)}, u32[]{:S(2)}) copy-start(f32[1,128]{1,0:T(1,128)} %get-tuple-element.5) | copy-start | bytes 1540

commit v3 on v2

--- a/solution.py
+++ b/solution.py
@@ -16,7 +16,7 @@
 GR = 2 * RB
 R = 16 * RB
 CH = 256
-Q = 4
+Q = 2
 QR = CH // Q
 SHARP = 4.0 / math.sqrt(W)
 C2 = SHARP / math.log(2.0)
@@ -277,7 +277,7 @@
         put("13", 2, q, piece(1, 3, q), mass, peer(dx=-1))
     weigh(0, 1)
     mass = local(0, 2)
-    for q in (0, 2, 1, 3):
+    for q in range(Q):
         total = piece(0, 2, q) + got("12", 0, q)
         if q == 0:
             mass = mass + got_mass(0)

time: 81.5 us -> 81.8 us (level)
  no operation moved by 1% of the time
where the time goes in v3:
time: 81.8 us; the launch traced here: 81.6 us
  Pallas kernels  80.5 us (98%)
    pallas_call x1, Pallas kernels, shards(): pl.pallas_call(kernel, out_shape=(jax.ShapeDtypeStruct((K, W), BF), jax.S...  75.7 us
    pallas_call x1, Pallas kernels, shards(): pl.pallas_call(decode_kernel, out_shape=jax.ShapeDtypeStruct((K, W), F32)...  4.76 us

profile of v3, /device:TPU:1, one launch (start us, length us, event | category | flops | bytes accessed | tf_op | source)
XLA Modules:
  0.0 81.6 jit_solution(15617177135203153063)
XLA Ops:
  0.6 75.7 %shard_map.41 = (bf16[4096,256]{1,0:T(8,128)(2,1)}, f32[1,128]{1,0:T(1,128)}) custom-call(bf16[128,256]{1,0:T(8,128)(2,1)} %points.1, f32[4096,256]{1,0:T(8,128)} %codebook.1), custom_call_target="tpu_custom_call" | custom-call | flops 8589934592 | bytes 8388608 | tf_op jit(solution)/shard_map/pallas_call | solution.py:360
  76.3 0.0 copy-start
  76.4 4.8 %shard_map.42 = f32[4096,256]{1,0:T(8,128)} custom-call(bf16[4096,256]{1,0:T(8,128)(2,1)} %get-tuple-element.4.coded), custom_call_target="tpu_custom_call" | custom-call | tf_op jit(solution)/shard_map/pallas_call | solution.py:394
  81.1 0.0 copy-done
  81.1 0.5 copy.5
Async XLA Ops:
  76.3 4.8 %copy-start = (f32[1,128]{1,0:T(1,128)S(1)}, f32[1,128]{1,0:T(1,128)}, u32[]{:S(2)}) copy-start(f32[1,128]{1,0:T(1,128)} %get-tuple-element.5) | copy-start | bytes 1540
